TPU v7x, 32 devices: a whole 2x2x4 slice. The times are simulated.
32 devices in a mesh: group: 2 (over x), row: 16 (over z, y, core).
Axes of the slice: x: 2, y: 2, z: 4, core: 2. Of those that a mesh axis runs over, the one named last changes fastest.
Arguments:
- factor_panel: bfloat16 [65536, 4096], P(('group', 'row')), parts along dimension 0, may hold values from -0.046875 to 0.046875
- right_side: float32 [65536, 256], P(('group', 'row')), parts along dimension 0, may hold values from -6 to 6
- solved_below: bfloat16 [65536, 256], P(('group', 'row')), parts along dimension 0, may hold values from -6 to 6
- diag_inverse: bfloat16 [32768, 1024], P(('group', 'row')), parts along dimension 0, may hold values from -1.5 to 1.5
Outputs:
- forward: float32 [65536, 256], P(('group', 'row')), parts along dimension 0
- solution: float32 [65536, 256], P(('group', 'row')), parts along dimension 0
There are 2 independent parts, one for each index of `group`. A program takes and returns all parts, laid end to end along the dimension named above; each array names one. Nothing has to cross between parts.
All inputs are finite; a program needn't handle non-finite values.
Results may differ from a plain program's by a relative error of at most 0.0021.
Values may be sent and summed in bfloat16 or wider, within the bound.
A program may use at most 128 MiB of HBM per device.

v0:
```python
import jax
import jax.numpy as jnp
from jax import lax
from jax.sharding import PartitionSpec as P


def from_root(block, axis, source):
    block = jnp.where(lax.axis_index(axis) == source, block, jnp.zeros_like(block))
    return lax.psum(block, axis)


def transposed(left, right):
    return lax.dot_general(
        left, right, (((0,), (0,)), ((), ())), preferred_element_type=jnp.float32
    )


def body(factor_panel, right_side, solved_below, diag_inverse):
    position = lax.axis_index("row")
    block = diag_inverse.shape[1]
    steps_count = factor_panel.shape[1] // block
    local_rows = jnp.arange(factor_panel.shape[0], dtype=jnp.int32)
    window_mask = jnp.logical_and(local_rows < block, position < steps_count)[:, None]
    known = jnp.where(window_mask, jnp.zeros_like(solved_below), solved_below)
    current = right_side
    forward_block = jnp.zeros((block, right_side.shape[1]), jnp.float32)
    for step in range(steps_count):
        columns = factor_panel[:, step * block : (step + 1) * block]
        solved = lax.cond(
            position == step,
            lambda values: jnp.dot(
                diag_inverse, values.astype(jnp.bfloat16), preferred_element_type=jnp.float32
            ),
            lambda values: jnp.zeros_like(values),
            current[:block],
        )
        forward_block = jnp.where(position == step, solved, forward_block)
        shared = from_root(solved.astype(jnp.bfloat16), "row", step)
        current = current - jnp.dot(columns, shared, preferred_element_type=jnp.float32)
    forward = current.at[:block].set(
        jnp.where(position < steps_count, forward_block, current[:block])
    )
    own_solution = jnp.zeros_like(forward_block)
    for step in reversed(range(steps_count)):
        columns = factor_panel[:, step * block : (step + 1) * block]
        total = lax.psum(transposed(columns, known), "row")
        value = lax.cond(
            position == step,
            lambda sums: transposed(diag_inverse, (forward_block - sums).astype(jnp.bfloat16)),
            lambda sums: jnp.zeros_like(sums),
            total,
        )
        known = known.at[:block].set(
            jnp.where(position == step, value.astype(jnp.bfloat16), known[:block])
        )
        own_solution = jnp.where(position == step, value, own_solution)
    base = solved_below.astype(jnp.float32)
    solution = base.at[:block].set(jnp.where(position < steps_count, own_solution, base[:block]))
    return (forward, solution)


def solution(mesh):
    in_specs = (
        P(("group", "row"), None),
        P(("group", "row"), None),
        P(("group", "row"), None),
        P(("group", "row"), None),
    )
    out_specs = (P(("group", "row"), None), P(("group", "row"), None))
    return jax.shard_map(body, mesh=mesh, in_specs=in_specs, out_specs=out_specs, check_vma=False)
```

profile of v0, /device:TPU:30, one launch (start us, length us, event | category | flops | bytes accessed | tf_op | source)
XLA Modules:
  0.0 837.3 jit_solution(13086038905984973450)
XLA Ops:
  8.4 2.9 copy.7
  11.3 91.2 %all-reduce.9.cloned.1.call-done = bf16[1024,256]{0,1:T(8,128)(2,1)} async-done(((bf16[1024,256]{0,1:T(8,128)(2,1)}), bf16[1024,256]{0,1:T(8,128)(2,1)}) %all-reduce.9.cloned.1.call-update) | async-done | bytes 524304 | tf_op jit(solution)/shard_map/psum | solution.py:9
  102.5 5.6 fusion.41
  108.2 2.0 conditional.9
  111.6 1.4 copy.18
  113.0 93.3 %all-reduce.11.cloned.1.call-done = bf16[1024,256]{0,1:T(8,128)(2,1)} async-done(((bf16[1024,256]{0,1:T(8,128)(2,1)}), bf16[1024,256]{0,1:T(8,128)(2,1)}) %all-reduce.11.cloned.1.call-update) | async-done | bytes 524304 | tf_op jit(solution)/shard_map/psum | solution.py:9
  206.3 5.7 fusion.38
  211.9 1.9 conditional.10
  215.3 1.9 broadcast_select_fusion
  217.2 92.7 %all-reduce.13.cloned.1.call-done = bf16[1024,256]{0,1:T(8,128)(2,1)} async-done(((bf16[1024,256]{0,1:T(8,128)(2,1)}), bf16[1024,256]{0,1:T(8,128)(2,1)}) %all-reduce.13.cloned.1.call-update) | async-done | bytes 524304 | tf_op jit(solution)/shard_map/psum | solution.py:9
  309.8 5.6 fusion.35
  315.5 2.1 conditional.11
  318.5 4.8 fusion.53
  323.5 90.1 %all-reduce.15.cloned.1.call-done = bf16[1024,256]{0,1:T(8,128)(2,1)} async-done(((bf16[1024,256]{0,1:T(8,128)(2,1)}), bf16[1024,256]{0,1:T(8,128)(2,1)}) %all-reduce.15.cloned.1.call-update) | async-done | bytes 524304 | tf_op jit(solution)/shard_map/psum | solution.py:9
  413.7 5.7 fusion.32
  419.4 2.8 fusion.57
  422.1 87.6 %all-reduce.17.cloned.1.call-done = f32[1024,256]{0,1:T(8,128)} async-done(((f32[1024,256]{0,1:T(8,128)}), f32[1024,256]{0,1:T(8,128)}) %all-reduce.17.cloned.1.call-update) | async-done | bytes 1048592 | tf_op jit(solution)/shard_map/psum | solution.py:46
  509.7 2.0 conditional.12
  511.7 2.4 constant_dynamic-update-slice_fusion
  514.1 4.7 fusion.50
  518.9 95.1 %all-reduce.19.cloned.1.call-done = f32[1024,256]{0,1:T(8,128)} async-done(((f32[1024,256]{0,1:T(8,128)}), f32[1024,256]{0,1:T(8,128)}) %all-reduce.19.cloned.1.call-update) | async-done | bytes 1048592 | tf_op jit(solution)/shard_map/psum | solution.py:46
  614.0 1.9 conditional.13
  615.9 2.1 fusion.58
  618.0 4.7 fusion.47
  622.8 96.7 %all-reduce.21.cloned.1.call-done = f32[1024,256]{0,1:T(8,128)} async-done(((f32[1024,256]{0,1:T(8,128)}), f32[1024,256]{0,1:T(8,128)}) %all-reduce.21.cloned.1.call-update) | async-done | bytes 1048592 | tf_op jit(solution)/shard_map/psum | solution.py:46
  719.5 2.0 conditional.14
  721.5 2.1 select_dynamic-update-slice_fusion
  723.7 4.8 fusion.44
  728.5 2.9 copy.28
  731.4 92.3 %all-reduce.23.cloned.1.call-done = f32[1024,256]{0,1:T(8,128)} async-done(((f32[1024,256]{0,1:T(8,128)}), f32[1024,256]{0,1:T(8,128)}) %all-reduce.23.cloned.1.call-update) | async-done | bytes 1048592 | tf_op jit(solution)/shard_map/psum | solution.py:46
  824.7 2.9 fusion.56
  827.6 2.9 copy.29
  (48 shorter events, 19.7 us)
Async XLA Ops:
  7.2 95.4 %all-reduce.9.cloned.1.call-start = ((), (), s32[]{:S(2)}) async-start(), calls=%async_computation | async-start | bytes 1048576 | tf_op jit(solution)/shard_map/psum | solution.py:9
  7.4 3.9 copy-start.2
  8.4 197.9 %all-reduce.11.cloned.1.call-start = ((), (), s32[]{:S(2)}) async-start(), calls=%async_computation.1 | async-start | bytes 1048576 | tf_op jit(solution)/shard_map/psum | solution.py:9
  11.3 96.9 %copy-start = (bf16[1024,1024]{1,0:T(8,128)(2,1)S(1)}, bf16[1024,1024]{1,0:T(8,128)(2,1)}, u32[]{:S(2)}) copy-start(bf16[1024,1024]{1,0:T(8,128)(2,1)} %param.33) | copy-start | bytes 6291460
  110.1 1.4 copy-start.4
  111.0 198.8 %all-reduce.13.cloned.1.call-start = ((), (), s32[]{:S(2)}) async-start(), calls=%async_computation.2 | async-start | bytes 1048576 | tf_op jit(solution)/shard_map/psum | solution.py:9
  213.9 1.4 copy-start.1
  214.7 198.9 %all-reduce.15.cloned.1.call-start = ((), (), s32[]{:S(2)}) async-start(), calls=%async_computation.3 | async-start | bytes 1048576 | tf_op jit(solution)/shard_map/psum | solution.py:9
  318.5 191.2 %all-reduce.17.cloned.1.call-start = ((), (), s32[]{:S(2)}) async-start(), calls=%async_computation.4 | async-start | bytes 2097152 | tf_op jit(solution)/shard_map/psum | solution.py:46
  323.3 290.7 %all-reduce.19.cloned.1.call-start = ((), (), s32[]{:S(2)}) async-start(), calls=%async_computation.5 | async-start | bytes 2097152 | tf_op jit(solution)/shard_map/psum | solution.py:46
  413.7 5.7 copy-start.3
  518.8 200.7 %all-reduce.21.cloned.1.call-start = ((), (), s32[]{:S(2)}) async-start(), calls=%async_computation.6 | async-start | bytes 2097152 | tf_op jit(solution)/shard_map/psum | solution.py:46
  622.7 200.9 %all-reduce.23.cloned.1.call-start = ((), (), s32[]{:S(2)}) async-start(), calls=%async_computation.7 | async-start | bytes 2097152 | tf_op jit(solution)/shard_map/psum | solution.py:46
Sparse Core Ops, SparseCore 0:
  12.0 90.4 all-reduce.8
  111.1 95.0 all-reduce.10
  214.9 94.9 all-reduce.12
  318.6 95.0 all-reduce.14
  417.0 92.7 all-reduce.16
  519.0 94.9 all-reduce.18
  622.9 96.5 all-reduce.20
  728.6 94.9 all-reduce.22
where the time goes:
time: 848 us; the launch traced here: 837 us
  waiting for transfers between devices  739 us (87%)
  matrix products  41.6 us (5%)
  local copies, waits for them, and re-layouts  24.3 us (3%)
  other arithmetic  17.6 us (2%)
  between operations  14.2 us (2%)
    psum x4, waiting for transfers between devices, body(): total = lax.psum(transposed(columns, known), 'row')  372 us
    psum x4, waiting for transfers between devices, from_root(): return lax.psum(block, axis)  367 us
    dot_general x4, matrix products, body(): jnp.dot(columns, shared, preferred_element_type=jnp.float32)  22.7 us
    dot_general x4, matrix products, transposed(): lax.dot_general(left, right, (((0,), (0,)), ((), ())), preferred_element_...  19 us
  transfers between devices with their start and end apart: 8, of which 8 were waited for; matrix products, arithmetic and copies ran while one was open for 3% of the time, Pallas kernels for 0%

commit v1 on v0

v1 whole, which is shorter than its diff:
```python
import functools

import jax
import jax.numpy as jnp
from jax import lax
from jax.experimental import pallas as pl
from jax.experimental.pallas import tpu as pltpu
from jax.sharding import PartitionSpec as P

F32 = jnp.float32
BF16 = jnp.bfloat16
NC = 4


def dot(a, b):
    return jnp.dot(a, b, preferred_element_type=F32)


def kernel(
    n, wb, l_hbm, rs_hbm, sb_hbm, d_hbm, fwd_hbm, sol_hbm,
    lv, cur, sb, sbt, dv, sol, keep, cstage, crecv, ysend, yrecv, zsend, zrecv,
    yb, cbf, vt, xt, ca, caf, cb, cbs,
    ld_sem, lf_sem, cs_sem, cr_sem, ys_sem, yr_sem, zs_sem, zr_sem, bs_sem, br_sem,
    cas_sem, car_sem, cbs_sem, cbr_sem,
):
    me = lax.axis_index("row")
    nq = n // wb
    q = me // wb
    j = me % wb
    j1 = j + 1 - 2 * (j % 2)
    j2 = (j + 2) % wb
    j3 = (j1 + 2) % wb
    base = me - j
    block = dv.shape[0]
    ck = block // NC
    rows = cur.shape[0]
    tiles = rows // ck

    def span(start, size=None):
        return pl.ds(pl.multiple_of(start, ck), ck if size is None else size)

    def loop(lo, hi, f):
        def step(i, _):
            f(i)
            return 0
        lax.fori_loop(lo, hi, step, 0)

    def remote(src, dst, ssem, rsem, to):
        return pltpu.make_async_remote_copy(
            src_ref=src, dst_ref=dst, send_sem=ssem, recv_sem=rsem,
            device_id={"row": to}, device_id_type=pl.DeviceIdType.MESH,
        )

    ld_d = pltpu.make_async_copy(d_hbm, dv, ld_sem.at[0])
    ld_r = pltpu.make_async_copy(rs_hbm, cur, ld_sem.at[1])
    ld_s = pltpu.make_async_copy(sb_hbm, sb, ld_sem.at[2])
    out_f = pltpu.make_async_copy(cur, fwd_hbm, ld_sem.at[3])
    out_s = pltpu.make_async_copy(sol, sol_hbm, ld_sem.at[4])

    def ld_l(h, b, c):
        where = (pl.ds(h * block, rows - block if h else block), span(b * block + c * ck))
        return pltpu.make_async_copy(l_hbm.at[where], lv.at[where], lf_sem.at[h, b, c])

    ld_r.start()
    ld_d.start()
    ld_s.start()
    loop(0, NC, lambda c: ld_l(0, 0, c).start())

    def load_rest(c):
        for b in range(wb):
            if b:
                ld_l(0, b, c).start()
            ld_l(1, b, c).start()
    loop(0, NC, load_rest)

    barrier = pltpu.get_barrier_semaphore()

    def greet(to):
        pl.semaphore_signal(barrier, inc=1, device_id={"row": to}, device_id_type=pl.DeviceIdType.MESH)

    greet(base + j1)
    greet(base + j2)
    greet(base + j3)

    @pl.when(q > 0)
    def _():
        greet(me - wb)

    @pl.when(q < nq - 1)
    def _():
        greet(me + wb)

    pl.semaphore_wait(barrier, 3 + jnp.where(q > 0, 1, 0) + jnp.where(q < nq - 1, 1, 0))

    def y_copy(way, k, c, to):
        part = yb.at[k, span(c * ck)]
        return remote(part, part, bs_sem.at[way, k, c], br_sem.at[k, c], to)

    def y_each(k, c, act):
        @pl.when(j % 2 == k % 2)
        def _():
            @pl.when((q == 0) & (j == k))
            def _():
                act(y_copy(1, k, c, base + j2))
            act(y_copy(0, k, c, base + j1))

            @pl.when(q < nq - 1)
            def _():
                act(y_copy(2, k, c, me + wb))

    def y_send(k, c):
        y_each(k, c, lambda copy: copy.start())

    def y_get(k, c):
        y_copy(0, k, c, base + j1).wait_recv()
        y_send(k, c)

    def get(k):
        loop(0, NC, lambda c: y_get(k, c))

    def absorb(k):
        def one(c):
            y_get(k, c)
            part = yb[k, span(c * ck)]

            def tile(t):
                r = span(t * ck)
                cur[r] = cur[r] - dot(lv[r, span(k * block + c * ck)], part)
            loop(0, NC, tile)
        loop(0, NC, one)

    def produce(k):
        cbf[...] = cur[0:block].astype(BF16)

        def one(c):
            r = span(c * ck)
            y = dot(dv[r], cbf[...])
            cur[r] = y
            yb[k, r] = y.astype(BF16)
            y_send(k, c)
        loop(0, NC, one)

    ld_r.wait()
    ld_d.wait()

    @pl.when(me == 0)
    def _():
        produce(0)

    loop(0, NC, lambda c: ld_l(0, 0, c).wait())

    @pl.when(me == 1)
    def _():
        absorb(0)
        produce(1)

    ld_s.wait()

    def turn(t):
        r = span(t * ck)
        x = sb[r].astype(F32)
        sol[r] = x
        first = (q == 0) & (t < NC)
        sbt[:, r] = jnp.where(first, jnp.zeros_like(x), x).T.astype(BF16)
    loop(0, tiles, turn)

    @pl.when(q > 0)
    def _():
        out_s.start()

    def c_copy(s, c):
        return remote(cstage.at[s, c], crecv.at[s, c], cs_sem.at[s, c], cr_sem.at[s, c], base + j1)

    def y_part(c):
        return remote(ysend.at[c], yrecv.at[c], ys_sem.at[c], yr_sem.at[c], base + j2)

    def z_copy(c, to):
        return remote(zsend.at[c], zrecv.at[c], zs_sem.at[c], zr_sem.at[c], to)

    def cross(c):
        c_copy(1, c).wait_recv()
        ysend[c] = (keep[1, c] + crecv[1, c].astype(F32)).astype(ysend.dtype)
        y_part(c).start()

    def partial(c):
        for b in range(wb):
            if b:
                ld_l(0, b, c).wait()
            ld_l(1, b, c).wait()

        def other(s):
            b = (j1 + 2 * s) % wb
            cstage[s, c] = dot(sbt[...], lv[:, span(b * block + c * ck)]).astype(cstage.dtype)
            c_copy(s, c).start()

        def own(s):
            b = (j + 2 * s) % wb
            keep[s, c] = dot(sbt[...], lv[:, span(b * block + c * ck)])
        loop(0, 2, lambda s: other(1 - s))
        loop(0, 2, lambda s: own(1 - s))
        cross(c)
    loop(0, NC, partial)

    @pl.when(me == 2)
    def _():
        absorb(0)
        absorb(1)
        produce(2)

    @pl.when(me == 3)
    def _():
        absorb(0)
        absorb(1)
        absorb(2)
        produce(3)

    def gemm(k):
        def tile(t):
            r = span(t * ck)
            cur[r] = cur[r] - dot(lv[r, k * block:(k + 1) * block], yb[k])
        loop(jnp.where(q == 0, NC, 0), tiles, tile)

    def tail(c):
        c_copy(0, c).wait_recv()
        total = keep[0, c] + crecv[0, c].astype(F32)
        y_part(c).wait_recv()
        keep[0, c] = total + yrecv[c].astype(F32)

        @pl.when(q < nq - 1)
        def _():
            z_copy(c, me + wb).wait_recv()
            keep[0, c] = keep[0, c] + zrecv[c].astype(F32)

        @pl.when(q > 0)
        def _():
            zsend[c] = keep[0, c].astype(zsend.dtype)
            z_copy(c, me - wb).start()

    def ca_copy(slot, c, to):
        return remote(caf.at[slot, c], ca.at[slot, c], cas_sem.at[slot, c], car_sem.at[slot, c], to)

    def cb_copy(slot, c, to):
        return remote(cbs.at[slot, c], cb.at[c], cbs_sem.at[slot, c], cbr_sem.at[c], to)

    def back(k):
        def rhs(c):
            s = keep[0, c]
            if k == 2:
                ca_copy(2, c, base + j1).wait_recv()
                s = s + ca[2, c]
            if k < 2:
                cb_copy(0, c, base + 2).wait_recv()
                s = s + cb[c].astype(F32)
            if k == 0:
                ca_copy(0, c, base + j1).wait_recv()
                s = s + ca[0, c]
            vt[:, span(c * ck)] = (cur[span(c * ck)].T - s).astype(BF16)
        loop(0, NC, rhs)

        def solve(c):
            x = dot(vt[...], dv[:, span(c * ck)])
            xt[:, span(c * ck)] = x.astype(BF16)
            sol[span(c * ck)] = x.T
        loop(0, NC, solve)
        for kk in reversed(range(k)):
            def give(c):
                value = dot(xt[...], lv[0:block, span(kk * block + c * ck)])
                if k == 2:
                    ca_copy(kk, c, base + j1).wait_recv()
                    cbs[kk, c] = (value + ca[kk, c]).astype(cbs.dtype)
                    cb_copy(kk, c, base + kk).start()
                else:
                    caf[kk, c] = value
                    ca_copy(kk, c, base + j1).start()
            loop(0, NC, give)
        out_s.start()

    @pl.when(q > 0)
    def _():
        loop(0, NC, tail)
        for k in range(wb):
            get(k)
            gemm(k)
        out_f.start()

    @pl.when(me == 0)
    def _():
        gemm(0)
        get(1)
        gemm(1)

    @pl.when(me == 1)
    def _():
        gemm(0)
        gemm(1)

    @pl.when(q == 0)
    def _():
        loop(0, NC, tail)

        @pl.when(j < 2)
        def _():
            for k in (2, 3):
                get(k)
                gemm(k)
            out_f.start()

        @pl.when(j == 0)
        def _():
            back(0)

        @pl.when(j == 1)
        def _():
            back(1)

        @pl.when(j == 2)
        def _():
            back(2)
            get(3)

        @pl.when(j == 3)
        def _():
            back(3)

        @pl.when(j >= 2)
        def _():
            for k in range(wb):
                gemm(k)
            out_f.start()

    def finish(c):
        c_copy(0, c).wait_send()
        c_copy(1, c).wait_send()
        y_part(c).wait_send()

        @pl.when(q > 0)
        def _():
            z_copy(c, me - wb).wait_send()
        for k in range(wb):
            y_each(k, c, lambda copy: copy.wait_send())

        @pl.when(me == 3)
        def _():
            for kk in range(3):
                ca_copy(kk, c, base + j1).wait_send()

        @pl.when(me == 2)
        def _():
            for kk in range(2):
                cb_copy(kk, c, base + kk).wait_send()

        @pl.when(me == 1)
        def _():
            ca_copy(0, c, base + j1).wait_send()
    loop(0, NC, finish)
    out_f.wait()
    out_s.wait()


def body(n, factor_panel, right_side, solved_below, diag_inverse):
    rows, width = factor_panel.shape
    block = diag_inverse.shape[1]
    wb = width // block
    cols = right_side.shape[1]
    ck = block // NC
    piece = (NC, cols, ck)
    dma = pltpu.SemaphoreType.DMA
    out = jax.ShapeDtypeStruct(right_side.shape, F32)
    return tuple(pl.pallas_call(
        functools.partial(kernel, n, wb),
        out_shape=(out, out),
        in_specs=[pl.BlockSpec(memory_space=pl.ANY)] * 4,
        out_specs=(pl.BlockSpec(memory_space=pl.ANY),) * 2,
        scratch_shapes=[
            pltpu.VMEM((rows, width), BF16),
            pltpu.VMEM((rows, cols), F32),
            pltpu.VMEM((rows, cols), BF16),
            pltpu.VMEM((cols, rows), BF16),
            pltpu.VMEM((block, block), BF16),
            pltpu.VMEM((rows, cols), F32),
            pltpu.VMEM((2,) + piece, F32),
            pltpu.VMEM((2,) + piece, F32),
            pltpu.VMEM((2,) + piece, F32),
            pltpu.VMEM(piece, BF16),
            pltpu.VMEM(piece, BF16),
            pltpu.VMEM(piece, F32),
            pltpu.VMEM(piece, F32),
            pltpu.VMEM((wb, block, cols), BF16),
            pltpu.VMEM((block, cols), BF16),
            pltpu.VMEM((cols, block), BF16),
            pltpu.VMEM((cols, block), BF16),
            pltpu.VMEM((3,) + piece, F32),
            pltpu.VMEM((3,) + piece, F32),
            pltpu.VMEM(piece, BF16),
            pltpu.VMEM((2,) + piece, BF16),
            dma((5,)), dma((2, wb, NC)),
            dma((2, NC)), dma((2, NC)),
            dma((NC,)), dma((NC,)), dma((NC,)), dma((NC,)),
            dma((3, wb, NC)), dma((wb, NC)),
            dma((3, NC)), dma((3, NC)), dma((2, NC)), dma((NC,)),
        ],
        compiler_params=pltpu.CompilerParams(
            collective_id=0, has_side_effects=True, vmem_limit_bytes=60 * 1024 * 1024
        ),
        cost_estimate=pl.CostEstimate(
            flops=4 * rows * width * cols, bytes_accessed=2 * rows * width, transcendentals=0
        ),
    )(factor_panel, right_side, solved_below, diag_inverse))


def solution(mesh):
    spec = P(("group", "row"), None)
    return jax.shard_map(
        functools.partial(body, mesh.shape["row"]),
        mesh=mesh, in_specs=(spec,) * 4, out_specs=(spec,) * 2, check_vma=False,
    )
```

time: 848 us -> 88.9 us (0.10); the launches traced: 837 us -> 88.8 us
  waiting for transfers between devices: 739 us -> 0 us
  Pallas kernels: 0 us -> 83.6 us
  matrix products: 41.6 us -> 0 us
  local copies, waits for them, and re-layouts: 24.3 us -> 4.52 us
  other arithmetic: 17.6 us -> 0 us
  between operations: 14.2 us -> 0.65 us
    psum x8 -> x0, waiting for transfers between devices: 739 us -> none  [the longest x4 372 us: body(): total = lax.psum(transposed(columns, known), 'row')]
    pallas_call x0 -> x1, Pallas kernels: none -> 83.6 us  [body(): pl.pallas_call(functools.partial(kernel, n, wb), out_shape=(out, out), in...]
    dot_general x8 -> x0, matrix products: 41.6 us -> none  [the longest x4 22.7 us: body(): jnp.dot(columns, shared, preferred_element_type=jnp.float32)]
    another operation x15 -> x0, local copies, waits for them, and re-layouts: 13.2 us -> none
    scatter x5 -> x0, other arithmetic: 12.2 us -> none  [the longest x3 6.58 us: body(): known.at[:block]]
  transfers between devices with their start and end apart: 8 -> 0, of which waited for: 8 -> 0; matrix products, arithmetic and copies ran while one was open for 3% -> 0% of each run, Pallas kernels for 0% -> 0%
where the time goes in v1:
time: 88.9 us; the launch traced here: 88.8 us
  Pallas kernels  83.6 us (94%)
  local copies, waits for them, and re-layouts  4.52 us (5%)
    pallas_call x1, Pallas kernels, body(): pl.pallas_call(functools.partial(kernel, n, wb), out_shape=(out, out), in...  83.6 us
    unnamed x4, local copies, waits for them, and re-layouts  4.52 us

profile of v1, /device:TPU:30, one launch (start us, length us, event | category | flops | bytes accessed | tf_op | source)
XLA Modules:
  0.0 88.8 jit_solution(13698718179817657695)
XLA Ops:
  0.6 83.6 %shard_map.59 = (f32[2048,256]{1,0:T(8,128)}, f32[2048,256]{1,0:T(8,128)}) custom-call(bf16[2048,4096]{1,0:T(8,128)(2,1)} %l_hbm.1, f32[2048,256]{1,0:T(8,128)} %rs_hbm.1, bf16[2048,256]{1,0:T(8,128)(2,1)} %sb_hbm.1, bf16[1024,1024]{1,0:T(8,128)(2,1)} %d_hbm.1), custom_call_target="tpu_custom_call" | custom-call | flops 8589934592 | bytes 16777216 | tf_op jit(solution)/shard_map/pallas_call | solution.py:369
  84.3 0.0 copy-start
  84.3 3.2 %copy.8 = f32[2048,256]{1,0:T(8,128)} copy(f32[2048,256]{1,0:T(8,128)} %get-tuple-element.4) | data formatting | bytes 4194304
  87.5 0.0 copy-done
  87.5 1.3 %copy.9 = f32[2048,256]{1,0:T(8,128)} copy(f32[2048,256]{1,0:T(8,128)S(1)} %copy-done) | data formatting | bytes 4194304
Async XLA Ops:
  84.3 3.2 %copy-start = (f32[2048,256]{1,0:T(8,128)S(1)}, f32[2048,256]{1,0:T(8,128)}, u32[]{:S(2)}) copy-start(f32[2048,256]{1,0:T(8,128)} %get-tuple-element.5) | copy-start | bytes 6291460

commit v2 on v1

--- a/solution.py
+++ b/solution.py
@@ -10,6 +10,7 @@
 F32 = jnp.float32
 BF16 = jnp.bfloat16
 NC = 4
+NF = 2
 
 
 def dot(a, b):
@@ -19,7 +20,7 @@
 def kernel(
     n, wb, l_hbm, rs_hbm, sb_hbm, d_hbm, fwd_hbm, sol_hbm,
     lv, cur, sb, sbt, dv, sol, keep, cstage, crecv, ysend, yrecv, zsend, zrecv,
-    yb, cbf, vt, xt, ca, caf, cb, cbs,
+    zsend_b, zrecv_b, yb, cbf, vt, xt, ca, caf, cb, cbs,
     ld_sem, lf_sem, cs_sem, cr_sem, ys_sem, yr_sem, zs_sem, zr_sem, bs_sem, br_sem,
     cas_sem, car_sem, cbs_sem, cbr_sem,
 ):
@@ -64,6 +65,25 @@
     ld_r.start()
     ld_d.start()
     ld_s.start()
+    barrier = pltpu.get_barrier_semaphore()
+
+    def greet(to):
+        pl.semaphore_signal(barrier, inc=1, device_id={"row": to}, device_id_type=pl.DeviceIdType.MESH)
+
+    greet(base + j1)
+    greet(base + j2)
+    greet(base + j3)
+
+    @pl.when(q > 0)
+    def _():
+        greet(me - wb)
+
+    @pl.when(q < nq - 1)
+    def _():
+        greet(me + wb)
+
+    pl.semaphore_wait(barrier, 3 + jnp.where(q > 0, 1, 0) + jnp.where(q < nq - 1, 1, 0))
+
     loop(0, NC, lambda c: ld_l(0, 0, c).start())
 
     def load_rest(c):
@@ -73,25 +93,6 @@
             ld_l(1, b, c).start()
     loop(0, NC, load_rest)
 
-    barrier = pltpu.get_barrier_semaphore()
-
-    def greet(to):
-        pl.semaphore_signal(barrier, inc=1, device_id={"row": to}, device_id_type=pl.DeviceIdType.MESH)
-
-    greet(base + j1)
-    greet(base + j2)
-    greet(base + j3)
-
-    @pl.when(q > 0)
-    def _():
-        greet(me - wb)
-
-    @pl.when(q < nq - 1)
-    def _():
-        greet(me + wb)
-
-    pl.semaphore_wait(barrier, 3 + jnp.where(q > 0, 1, 0) + jnp.where(q < nq - 1, 1, 0))
-
     def y_copy(way, k, c, to):
         part = yb.at[k, span(c * ck)]
         return remote(part, part, bs_sem.at[way, k, c], br_sem.at[k, c], to)
@@ -122,11 +123,7 @@
         def one(c):
             y_get(k, c)
             part = yb[k, span(c * ck)]
-
-            def tile(t):
-                r = span(t * ck)
-                cur[r] = cur[r] - dot(lv[r, span(k * block + c * ck)], part)
-            loop(0, NC, tile)
+            cur[0:block] = cur[0:block] - dot(lv[0:block, span(k * block + c * ck)], part)
         loop(0, NC, one)
 
     def produce(k):
@@ -146,6 +143,7 @@
     @pl.when(me == 0)
     def _():
         produce(0)
+        get(1)
 
     loop(0, NC, lambda c: ld_l(0, 0, c).wait())
 
@@ -177,10 +175,45 @@
     def z_copy(c, to):
         return remote(zsend.at[c], zrecv.at[c], zs_sem.at[c], zr_sem.at[c], to)
 
+    def z_copy_b(c, to):
+        return remote(zsend_b.at[c], zrecv_b.at[c], zs_sem.at[c], zr_sem.at[c], to)
+
     def cross(c):
         c_copy(1, c).wait_recv()
         ysend[c] = (keep[1, c] + crecv[1, c].astype(F32)).astype(ysend.dtype)
         y_part(c).start()
+
+    last = q == nq - 1
+
+    def tail(c):
+        c_copy(0, c).wait_recv()
+        total = keep[0, c] + crecv[0, c].astype(F32)
+        y_part(c).wait_recv()
+        keep[0, c] = total + yrecv[c].astype(F32)
+
+        @pl.when(q < nq - 1)
+        def _():
+            @pl.when(c < NF)
+            def _():
+                z_copy(c, me + wb).wait_recv()
+                keep[0, c] = keep[0, c] + zrecv[c]
+
+            @pl.when(c >= NF)
+            def _():
+                z_copy_b(c, me + wb).wait_recv()
+                keep[0, c] = keep[0, c] + zrecv_b[c].astype(F32)
+
+        @pl.when(q > 0)
+        def _():
+            @pl.when(c < NF)
+            def _():
+                zsend[c] = keep[0, c]
+                z_copy(c, me - wb).start()
+
+            @pl.when(c >= NF)
+            def _():
+                zsend_b[c] = keep[0, c].astype(BF16)
+                z_copy_b(c, me - wb).start()
 
     def partial(c):
         for b in range(wb):
@@ -199,6 +232,10 @@
         loop(0, 2, lambda s: other(1 - s))
         loop(0, 2, lambda s: own(1 - s))
         cross(c)
+
+        @pl.when(last & (c > 0))
+        def _():
+            tail(c - 1)
     loop(0, NC, partial)
 
     @pl.when(me == 2)
@@ -219,22 +256,6 @@
             r = span(t * ck)
             cur[r] = cur[r] - dot(lv[r, k * block:(k + 1) * block], yb[k])
         loop(jnp.where(q == 0, NC, 0), tiles, tile)
-
-    def tail(c):
-        c_copy(0, c).wait_recv()
-        total = keep[0, c] + crecv[0, c].astype(F32)
-        y_part(c).wait_recv()
-        keep[0, c] = total + yrecv[c].astype(F32)
-
-        @pl.when(q < nq - 1)
-        def _():
-            z_copy(c, me + wb).wait_recv()
-            keep[0, c] = keep[0, c] + zrecv[c].astype(F32)
-
-        @pl.when(q > 0)
-        def _():
-            zsend[c] = keep[0, c].astype(zsend.dtype)
-            z_copy(c, me - wb).start()
 
     def ca_copy(slot, c, to):
         return remote(caf.at[slot, c], ca.at[slot, c], cas_sem.at[slot, c], car_sem.at[slot, c], to)
@@ -275,18 +296,46 @@
             loop(0, NC, give)
         out_s.start()
 
+    def carried(low, ours):
+        for k in (low, low + 1):
+            @pl.when((j % 2 == k % 2) if ours else (j % 2 != k % 2))
+            def _():
+                get(k)
+
     @pl.when(q > 0)
     def _():
-        loop(0, NC, tail)
-        for k in range(wb):
-            get(k)
-            gemm(k)
+        @pl.when((q == 1) & ~last)
+        def _():
+            carried(0, True)
+        loop(jnp.where(last, NC - 1, 0), NC // 2, tail)
+
+        @pl.when((q > 1) & ~last)
+        def _():
+            carried(0, True)
+        loop(jnp.where(last, NC - 1, NC // 2), NC, tail)
+
+        @pl.when(last)
+        def _():
+            carried(0, True)
+
+        @pl.when(~last)
+        def _():
+            carried(2, True)
+        carried(0, False)
+        gemm(0)
+        gemm(1)
+
+        @pl.when(last)
+        def _():
+            carried(2, True)
+        carried(2, False)
+        gemm(2)
+        gemm(3)
         out_f.start()
 
     @pl.when(me == 0)
     def _():
         gemm(0)
-        get(1)
         gemm(1)
 
     @pl.when(me == 1)
@@ -335,7 +384,13 @@
 
         @pl.when(q > 0)
         def _():
-            z_copy(c, me - wb).wait_send()
+            @pl.when(c < NF)
+            def _():
+                z_copy(c, me - wb).wait_send()
+
+            @pl.when(c >= NF)
+            def _():
+                z_copy_b(c, me - wb).wait_send()
         for k in range(wb):
             y_each(k, c, lambda copy: copy.wait_send())
 
@@ -381,10 +436,12 @@
             pltpu.VMEM((2,) + piece, F32),
             pltpu.VMEM((2,) + piece, F32),
             pltpu.VMEM((2,) + piece, F32),
+            pltpu.VMEM(piece, F32),
+            pltpu.VMEM(piece, F32),
+            pltpu.VMEM(piece, F32),
+            pltpu.VMEM(piece, F32),
             pltpu.VMEM(piece, BF16),
             pltpu.VMEM(piece, BF16),
-            pltpu.VMEM(piece, F32),
-            pltpu.VMEM(piece, F32),
             pltpu.VMEM((wb, block, cols), BF16),
             pltpu.VMEM((block, cols), BF16),
             pltpu.VMEM((cols, block), BF16),
@@ -400,7 +457,7 @@
             dma((3, NC)), dma((3, NC)), dma((2, NC)), dma((NC,)),
         ],
         compiler_params=pltpu.CompilerParams(
-            collective_id=0, has_side_effects=True, vmem_limit_bytes=60 * 1024 * 1024
+            collective_id=0, has_side_effects=True, vmem_limit_bytes=50 * 1024 * 1024
         ),
         cost_estimate=pl.CostEstimate(
             flops=4 * rows * width * cols, bytes_accessed=2 * rows * width, transcendentals=0

time: 88.9 us -> 80.3 us (0.903)
  the two profiles are of different devices: /device:TPU:30 before, /device:TPU:19 now
where the time goes in v2:
time: 80.3 us; the launch traced here: 80.1 us
  Pallas kernels  74.5 us (93%)
  local copies, waits for them, and re-layouts  4.88 us (6%)
    pallas_call x1, Pallas kernels, body(): pl.pallas_call(functools.partial(kernel, n, wb), out_shape=(out, out), in...  74.5 us
    unnamed x6, local copies, waits for them, and re-layouts  4.88 us

profile of v2, /device:TPU:19, one launch (start us, length us, event | category | flops | bytes accessed | tf_op | source)
XLA Modules:
  0.0 80.1 jit_solution(9892892511282281998)
XLA Ops:
  0.6 0.0 copy-start
  0.6 1.2 %copy-done = bf16[2048,256]{1,0:T(8,128)(2,1)S(1)} copy-done((bf16[2048,256]{1,0:T(8,128)(2,1)S(1)}, bf16[2048,256]{1,0:T(8,128)(2,1)}, u32[]{:S(2)}) %copy-start) | copy-done | bytes 1048600
  1.9 74.5 %shard_map.59 = (f32[2048,256]{1,0:T(8,128)S(1)}, f32[2048,256]{1,0:T(8,128)}) custom-call(bf16[2048,4096]{1,0:T(8,128)(2,1)} %l_hbm.1, f32[2048,256]{1,0:T(8,128)} %rs_hbm.1, bf16[2048,256]{1,0:T(8,128)(2,1)S(1)} %copy-done, bf16[1024,1024]{1,0:T(8,128)(2,1)} %d_hbm.1), custom_call_target="tpu_custom_call" | custom-call | flops 8589934592 | bytes 16777216 | tf_op jit(solution)/shard_map/pallas_call | solution.py:424
  76.4 0.0 copy-start.1
  76.4 1.3 %copy.8 = f32[2048,256]{1,0:T(8,128)} copy(f32[2048,256]{1,0:T(8,128)S(1)} %get-tuple-element.4) | data formatting | bytes 4194304
  77.7 1.0 %copy-done.1 = f32[2048,256]{1,0:T(8,128)S(1)} copy-done((f32[2048,256]{1,0:T(8,128)S(1)}, f32[2048,256]{1,0:T(8,128)}, u32[]{:S(2)}) %copy-start.1) | copy-done | bytes 2097176
  78.7 1.3 %copy.9 = f32[2048,256]{1,0:T(8,128)} copy(f32[2048,256]{1,0:T(8,128)S(1)} %copy-done.1) | data formatting | bytes 4194304
Async XLA Ops:
  0.6 1.2 %copy-start = (bf16[2048,256]{1,0:T(8,128)(2,1)S(1)}, bf16[2048,256]{1,0:T(8,128)(2,1)}, u32[]{:S(2)}) copy-start(bf16[2048,256]{1,0:T(8,128)(2,1)} %sb_hbm.1) | copy-start | bytes 3145732
  76.4 2.3 %copy-start.1 = (f32[2048,256]{1,0:T(8,128)S(1)}, f32[2048,256]{1,0:T(8,128)}, u32[]{:S(2)}) copy-start(f32[2048,256]{1,0:T(8,128)} %get-tuple-element.5) | copy-start | bytes 6291460
